TPU v7x, 32 devices: a whole 2x2x4 slice. The times are simulated.
32 devices in a mesh: dp: 8 (over z, y), mp: 4 (over x, core).
Axes of the slice: x: 2, y: 2, z: 4, core: 2. Of those that a mesh axis runs over, the one named last changes fastest.
Arguments:
- samples: bfloat16 [6144, 8192], P('dp', 'mp'), may hold values from -6 to 6
- gain: float32 [8192], P('mp'), may hold values from 0.1 to 1.9
- left_blocks: bfloat16 [64, 128, 128], P('mp'), may hold values from -0.5 to 0.5
- gate_blocks: bfloat16 [64, 128, 128], P('mp'), may hold values from -0.5 to 0.5
- right_blocks: bfloat16 [64, 128, 128], P('mp'), may hold values from -0.5 to 0.5
- cotangent: bfloat16 [6144, 8192], P('dp', 'mp'), may hold values from -6 to 6
Outputs:
- grad_input: bfloat16 [6144, 8192], P('dp', 'mp')
- grad_left: float32 [64, 128, 128], P('mp')
- grad_gate: float32 [64, 128, 128], P('mp')
- grad_right: float32 [64, 128, 128], P('mp')
All inputs are finite; a program needn't handle non-finite values.
Results may differ from a plain program's by a relative error of at most 0.007.
Values may be sent and summed in bfloat16 or wider, within the bound.
A program may use at most 128 MiB of HBM per device.

v0:
```python
import jax
import jax.numpy as jnp
from jax import lax
from jax.sharding import PartitionSpec as P

W = 8192
BLOCK = 128
NBLK = 64


def body(samples, gain, left_blocks, gate_blocks, right_blocks, cotangent):
    rows, width_local = samples.shape
    nlocal = left_blocks.shape[0]
    xf = samples.astype(jnp.float32)
    squares = lax.psum(jnp.sum(xf * xf, axis=1), "mp")
    rstd = lax.rsqrt(squares / W + 1e-05)[:, None]
    xn = (xf * rstd * gain).astype(jnp.bfloat16).reshape(rows, nlocal, BLOCK)
    act_a = jnp.einsum("tic,icj->tij", xn, left_blocks, preferred_element_type=jnp.float32)
    act_g = jnp.einsum("tic,icj->tij", xn, gate_blocks, preferred_element_type=jnp.float32)
    silu_g = jax.nn.silu(act_g)
    gated = (act_a * silu_g).astype(jnp.bfloat16)
    outgoing = (
        gated.reshape(rows, nlocal, NBLK, 2).transpose(0, 2, 1, 3).reshape(rows, NBLK, 2 * nlocal)
    )
    cot_blocks = cotangent.reshape(rows, nlocal, BLOCK)
    grad_perm = jnp.einsum(
        "tkm,kcm->tkc", cot_blocks, right_blocks, preferred_element_type=jnp.float32
    ).astype(jnp.bfloat16)
    permuted = lax.all_to_all(outgoing, "mp", split_axis=1, concat_axis=2, tiled=True)
    right_local = jnp.einsum(
        "tkc,tkm->kcm", permuted, cot_blocks, preferred_element_type=jnp.float32
    )
    returned = lax.all_to_all(grad_perm, "mp", split_axis=2, concat_axis=1, tiled=True)
    grad_gated = (
        returned.reshape(rows, NBLK, nlocal, 2)
        .transpose(0, 2, 1, 3)
        .reshape(rows, nlocal, BLOCK)
        .astype(jnp.float32)
    )
    sigma = jax.nn.sigmoid(act_g)
    grad_a = (grad_gated * silu_g).astype(jnp.bfloat16)
    grad_g = (grad_gated * act_a * sigma * (1.0 + act_g * (1.0 - sigma))).astype(jnp.bfloat16)
    left_local = jnp.einsum("tic,tij->icj", xn, grad_a, preferred_element_type=jnp.float32)
    gate_local = jnp.einsum("tic,tij->icj", xn, grad_g, preferred_element_type=jnp.float32)
    grad_norm = jnp.einsum("tij,icj->tic", grad_a, left_blocks, preferred_element_type=jnp.float32)
    grad_norm = grad_norm + jnp.einsum(
        "tij,icj->tic", grad_g, gate_blocks, preferred_element_type=jnp.float32
    )
    scaled = grad_norm.reshape(rows, width_local) * gain
    inner = lax.psum(jnp.sum(scaled * xf, axis=1), "mp")
    mean_inner = (inner / W)[:, None]
    grad_input = (
        cotangent.astype(jnp.float32) + rstd * (scaled - xf * rstd * rstd * mean_inner)
    ).astype(jnp.bfloat16)
    left_total, gate_total, right_total = lax.psum((left_local, gate_local, right_local), "dp")
    return (grad_input, left_total, gate_total, right_total)


def solution(mesh):
    placed = (
        P("dp", "mp"),
        P("mp"),
        P("mp", None, None),
        P("mp", None, None),
        P("mp", None, None),
        P("dp", "mp"),
    )
    return jax.shard_map(
        body,
        mesh=mesh,
        in_specs=placed,
        out_specs=(P("dp", "mp"), P("mp", None, None), P("mp", None, None), P("mp", None, None)),
        check_vma=False,
    )
```

profile of v0, /device:TPU:0, one launch (start us, length us, event | category | flops | bytes accessed | tf_op | source)
XLA Modules:
  0.0 314.0 jit_solution(13078904411900799919)
XLA Ops:
  7.2 0.0 copy-start
  7.2 3.1 convert_bitcast_fusion.1
  10.3 3.4 %copy.60 = bf16[768,16,128]{0,1,2:T(8,128)(2,1)} copy(bf16[768,16,128]{0,2,1:T(8,128)(2,1)S(1)} %convert_bitcast_fusion.1) | data formatting | bytes 6291456 | tf_op jit(solution)/shard_map/convert_element_type | solution.py:28
  13.7 4.6 %all-to-all-start = ((bf16[768,16,128]{0,1,2:T(8,128)(2,1)}), bf16[768,16,128]{0,1,2:T(8,128)(2,1)}, u32[]{:S(2)}, u32[]{:S(2)}) async-start(bf16[768,16,128]{0,1,2:T(8,128)(2,1)} %copy.60), calls=%async_computation | async-start | bytes 6291456 | tf_op jit(solution)/shard_map/all_to_all | solution.py:33
  18.3 0.0 copy-start.7
  18.3 2.6 fusion.8
  20.9 35.8 %psum.35 = f32[768]{0:T(1024)S(1)} all-reduce(f32[768]{0:T(1024)S(1)} %fusion.8), channel_id=1, replica_groups=mesh['dp'=8,'mp'=4] {'mp'}, use_global_device_ids=true, to_apply=%region_1.0 | all-reduce | flops 768 | bytes 6144 | tf_op jit(solution)/shard_map/psum | solution.py:15
  56.7 0.0 copy-done.7
  56.7 4.3 %fusion.2 = bf16[768,2048]{1,0:T(8,128)(2,1)} fusion(bf16[768,2048]{1,0:T(8,128)(2,1)} %param.6, f32[2048]{0:T(1024)S(1)} %copy-done.7, f32[768]{0:T(1024)S(1)} %add_rsqrt_fusion), kind=kLoop, calls=%fused_computation.5 | loop fusion | flops 6291456 | bytes 6302720 | tf_op jit(solution)/shard_map/convert_element_type | solution.py:17
  61.1 4.7 %copy.85 = bf16[768,2048]{0,1:T(8,128)(2,1)} copy(bf16[768,2048]{1,0:T(8,128)(2,1)} %fusion.2) | data formatting | bytes 6291456 | tf_op jit(solution)/shard_map/reshape | solution.py:17
  65.8 0.0 copy-done.5
  65.8 5.6 %fusion.26 = f32[16,768,128]{1,2,0:T(8,128)} fusion(bf16[768,16,128]{0,2,1:T(8,128)(2,1)} %bitcast.85, bf16[16,128,128]{2,1,0:T(8,128)(2,1)S(1)} %copy-done.5), kind=kOutput, calls=%fused_computation.38 | convolution fusion | flops 402653184 | bytes 9961472 | tf_op jit(solution)/shard_map/tic,icj->tij/dot_general | solution.py:19
  71.4 0.0 all-to-all-done
  71.4 2.9 copy.61
  74.3 0.8 convert_bitcast_fusion
  75.1 6.3 %copy.62 = f32[768,4,16,32]{0,2,1,3:T(8,128)} copy(f32[768,4,16,32]{0,3,1,2:T(8,128)S(1)} %convert_bitcast_fusion) | data formatting | bytes 12582912 | tf_op jit(solution)/shard_map/convert_element_type | solution.py:38
  81.4 10.3 %copy.63 = f32[768,16,64,2]{0,3,2,1:T(2,128)} copy(f32[768,16,64,2]{0,2,3,1:T(8,128)} %bitcast.89) | data formatting | bytes 12582912 | tf_op jit(solution)/shard_map/convert_element_type | solution.py:38
  91.7 8.5 %reshape.38 = f32[768,16,128]{0,2,1:T(8,128)} reshape(f32[768,16,64,2]{0,3,2,1:T(2,128)} %copy.63) | data formatting | bytes 12582912 | tf_op jit(solution)/shard_map/convert_element_type | solution.py:38
  100.2 0.0 copy-done
  100.2 9.7 %fusion.13 = (bf16[768,16,128]{0,2,1:T(8,128)(2,1)}, bf16[768,16,128]{0,2,1:T(8,128)(2,1)}, bf16[768,16,128]{0,2,1:T(8,128)(2,1)}) fusion(f32[16,768,128]{1,2,0:T(8,128)} %fusion.26, f32[768,16,128]{0,2,1:T(8,128)} %reshape.38, bf16[768,16,128]{0,2,1:T(8,128)(2,1)} %bitcast.86, bf16[16,128,128]{2,1,0:T(8,128)(2,1)S(1)} %copy-done), kind=kOutput, calls=%fused_computation.19 | convolution fusion | flops 426246144 | bytes 25690112 | tf_op jit(solution)/shard_map/tic,icj->tij/dot_general | solution.py:18
  109.9 7.3 %reshape.36 = bf16[768,16,64,2]{0,3,2,1:T(2,128)(2,1)} reshape(bf16[768,16,128]{0,2,1:T(8,128)(2,1)} %get-tuple-element.7) | data formatting | bytes 6291456 | tf_op jit(solution)/shard_map/reshape | solution.py:23
  117.2 2.5 copy.75
  119.8 3.4 %copy.76 = bf16[768,64,32]{0,2,1:T(8,128)(2,1)} copy(bf16[768,64,32]{0,1,2:T(8,128)(2,1)S(1)} %bitcast.91) | data formatting | bytes 6291456 | tf_op jit(solution)/shard_map/reshape | solution.py:23
  123.2 4.7 %all-to-all-start.1 = ((bf16[768,64,32]{0,2,1:T(8,128)(2,1)}), bf16[768,64,32]{0,2,1:T(8,128)(2,1)}, u32[]{:S(2)}, u32[]{:S(2)}) async-start(bf16[768,64,32]{0,2,1:T(8,128)(2,1)} %copy.76), calls=%async_computation.1 | async-start | bytes 6291456 | tf_op jit(solution)/shard_map/all_to_all | solution.py:29
  127.8 0.0 all-reduce.3.cloned.1.call-start
  127.9 0.0 copy-start.1
  127.9 0.0 copy-start.2
  127.9 4.9 %fusion.28 = f32[16,128,128]{2,1,0:T(8,128)} fusion(bf16[768,16,128]{0,2,1:T(8,128)(2,1)} %bitcast.87, bf16[768,16,128]{0,2,1:T(8,128)(2,1)} %get-tuple-element.8), kind=kOutput, calls=%fused_computation.40 | convolution fusion | flops 402653184 | bytes 7340032 | tf_op jit(solution)/shard_map/tic,tij->icj/dot_general | solution.py:44
  132.8 0.0 copy-done.1
  132.8 0.0 copy-done.2
  132.8 2.0 fusion.27
  134.8 30.0 %all-to-all-done.1 = bf16[768,64,32]{0,2,1:T(8,128)(2,1)} async-done(((bf16[768,64,32]{0,2,1:T(8,128)(2,1)}), bf16[768,64,32]{0,2,1:T(8,128)(2,1)}, u32[]{:S(2)}, u32[]{:S(2)}) %all-to-all-start.1) | async-done | bytes 3145760 | tf_op jit(solution)/shard_map/all_to_all | solution.py:29
  164.8 2.3 copy.77
  167.1 0.5 copy-done.3
  167.6 2.0 fusion.18
  169.6 0.0 all-reduce.3.cloned.1.call-update
  169.6 0.0 copy-start.4
  169.7 3.0 fusion.29
  172.7 0.0 copy-done.4
  172.7 3.6 %convolution_add_fusion = f32[16,768,128]{1,2,0:T(8,128)} fusion(f32[16,768,128]{1,2,0:T(8,128)S(1)} %fusion.29, bf16[16,128,128]{2,1,0:T(8,128)(2,1)S(1)} %copy-done.5, bf16[768,16,128]{0,2,1:T(8,128)(2,1)S(1)} %copy-done.4), kind=kOutput, calls=%fused_computation.35 | convolution fusion | flops 404226048 | bytes 16252928 | tf_op jit(solution)/shard_map/tij,icj->tic/dot_general | solution.py:46
  176.3 7.1 %copy.70 = f32[768,2048]{1,0:T(8,128)} copy(f32[768,2048]{0,1:T(8,128)} %bitcast.90) | data formatting | bytes 12582912 | tf_op jit(solution)/shard_map/reshape | solution.py:49
  183.4 4.7 %fusion.9 = f32[768]{0:T(1024)S(1)} fusion(bf16[768,2048]{1,0:T(8,128)(2,1)} %param.6, f32[768,2048]{1,0:T(8,128)} %copy.70, f32[2048]{0:T(1024)S(1)} %copy-done.7), kind=kLoop, calls=%fused_computation.12 | loop fusion | flops 6290688 | bytes 9448448 | tf_op jit(solution)/shard_map/reduce_sum | solution.py:50
  188.0 6.1 %psum.36 = f32[768]{0:T(1024)S(1)} all-reduce(f32[768]{0:T(1024)S(1)} %fusion.9), channel_id=1, replica_groups=mesh['dp'=8,'mp'=4] {'mp'}, use_global_device_ids=true, to_apply=%region_3.4 | all-reduce | flops 768 | bytes 6144 | tf_op jit(solution)/shard_map/psum | solution.py:50
  194.1 7.0 %fusion.7 = bf16[768,2048]{1,0:T(8,128)(2,1)} fusion(bf16[768,2048]{1,0:T(8,128)(2,1)} %param.6, bf16[768,2048]{1,0:T(8,128)(2,1)} %param.11, f32[768,2048]{1,0:T(8,128)} %copy.70, f32[768]{0:T(1024)S(1)} %broadcast_multiply_fusion, f32[2048]{0:T(1024)S(1)} %copy-done.7, f32[768]{0:T(1024)S(1)} %add_rsqrt_fusion), kind=kLoop, calls=%fused_computation.10 | loop fusion | flops 15728640 | bytes 15742976 | tf_op jit(solution)/shard_map/convert_element_type | solution.py:54
  201.1 100.5 %all-reduce.3.cloned.1.call-done = (f32[16,128,128]{2,1,0:T(8,128)}, f32[16,128,128]{2,1,0:T(8,128)}, f32[16,128,128]{2,1,0:T(8,128)}) async-done(((f32[16,128,128]{2,1,0:T(8,128)}, f32[16,128,128]{2,1,0:T(8,128)}, f32[16,128,128]{2,1,0:T(8,128)}), (f32[16,128,128]{2,1,0:T(8,128)}, f32[16,128,128]{2,1,0:T(8,128)}, f32[16,128,128]{2,1,0:T(8,128)})) %all-reduce.3.cloned.1.call-update) | async-done | bytes 3145744 | tf_op jit(solution)/shard_map/psum | solution.py:55
  301.6 2.4 copy.100
  303.9 2.3 copy.101
  306.2 1.0 copy.102
  (6 shorter events, 0.0 us)
Async XLA Ops:
  7.2 93.0 %copy-start = (bf16[16,128,128]{2,1,0:T(8,128)(2,1)S(1)}, bf16[16,128,128]{2,1,0:T(8,128)(2,1)}, u32[]{:S(2)}) copy-start(bf16[16,128,128]{2,1,0:T(8,128)(2,1)} %param.8) | copy-start | bytes 1572868
  13.7 57.7 %all-to-all-start = ((bf16[768,16,128]{0,1,2:T(8,128)(2,1)}), bf16[768,16,128]{0,1,2:T(8,128)(2,1)}, u32[]{:S(2)}, u32[]{:S(2)}) async-start(bf16[768,16,128]{0,1,2:T(8,128)(2,1)} %copy.60), calls=%async_computation | async-start | bytes 6291456 | tf_op jit(solution)/shard_map/all_to_all | solution.py:33
  18.3 38.4 %copy-start.7 = (f32[2048]{0:T(1024)S(1)}, f32[2048]{0:T(1024)}, u32[]{:S(2)}) copy-start(f32[2048]{0:T(1024)} %param.7) | copy-start | bytes 24580
  61.1 4.7 %copy-start.5 = (bf16[16,128,128]{2,1,0:T(8,128)(2,1)S(1)}, bf16[16,128,128]{2,1,0:T(8,128)(2,1)}, u32[]{:S(2)}) copy-start(bf16[16,128,128]{2,1,0:T(8,128)(2,1)} %param.9) | copy-start | bytes 1572868
  123.2 41.7 %all-to-all-start.1 = ((bf16[768,64,32]{0,2,1:T(8,128)(2,1)}), bf16[768,64,32]{0,2,1:T(8,128)(2,1)}, u32[]{:S(2)}, u32[]{:S(2)}) async-start(bf16[768,64,32]{0,2,1:T(8,128)(2,1)} %copy.76), calls=%async_computation.1 | async-start | bytes 6291456 | tf_op jit(solution)/shard_map/all_to_all | solution.py:29
  127.8 173.7 %all-reduce.3.cloned.1.call-start = ((), (), s32[]{:S(2)}) async-start(), calls=%async_computation.2 | async-start | bytes 6291456 | tf_op jit(solution)/shard_map/psum | solution.py:55
  127.9 5.0 %copy-start.1 = (bf16[768,2048]{0,1:T(8,128)(2,1)S(1)}, bf16[768,2048]{0,1:T(8,128)(2,1)}, u32[]{:S(2)}) copy-start(bf16[768,2048]{0,1:T(8,128)(2,1)} %copy.85) | copy-start | bytes 9437188
  127.9 5.0 %copy-start.2 = (bf16[768,16,128]{0,2,1:T(8,128)(2,1)S(1)}, bf16[768,16,128]{0,2,1:T(8,128)(2,1)}, u32[]{:S(2)}) copy-start(bf16[768,16,128]{0,2,1:T(8,128)(2,1)} %get-tuple-element.9) | copy-start | bytes 9437188
  164.8 2.8 copy-start.3
  169.6 3.0 copy-start.4
  301.5 4.7 %copy-start.6 = (f32[16,128,128]{2,1,0:T(8,128)S(1)}, f32[16,128,128]{2,1,0:T(8,128)}, u32[]{:S(2)}) copy-start(f32[16,128,128]{2,1,0:T(8,128)} %get-tuple-element.13) | copy-start | bytes 3145732
Sparse Core Ops, SparseCore 0:
  169.8 131.7 all-reduce.2
where the time goes:
time: 315 us; the launch traced here: 314 us
  waiting for transfers between devices  131 us (42%)
  local copies, waits for them, and re-layouts  64.9 us (21%)
  blocking collectives  41.9 us (13%)
  matrix products  33.9 us (11%)
  other arithmetic  19.4 us (6%)
  between operations  14.1 us (4%)
  starting transfers between devices  9.32 us (3%)
    psum x1, waiting for transfers between devices, body(): lax.psum((left_local, gate_local, right_local), 'dp')  100 us
    psum x1, blocking collectives, body(): squares = lax.psum(jnp.sum(xf * xf, axis=1), 'mp')  35.8 us
    all_to_all x1, waiting for transfers between devices, body(): lax.all_to_all(outgoing, 'mp', split_axis=1, concat_axis=2, tiled=True)  30 us
    convert_element_type x3, local copies, waits for them, and re-layouts, body(): grad_gated = returned.reshape(rows, NBLK, nlocal, 2).transpose(0, 2, 1, 3...  25 us
    reshape x3, local copies, waits for them, and re-layouts, body(): gated.reshape(rows, nlocal, NBLK, 2).transpose(0, 2, 1, 3)  13.2 us
    dot_general x1, matrix products, body(): jnp.einsum('tic,icj->tij', xn, left_blocks, preferred_element_type=jnp.fl...  9.74 us
    reshape x1, local copies, waits for them, and re-layouts, body(): scaled = grad_norm.reshape(rows, width_local) * gain  7.07 us
    convert_element_type x1, other arithmetic, body(): grad_input = (cotangent.astype(jnp.float32) + rstd * (scaled - xf * rstd...  6.97 us
  transfers between devices with their start and end apart: 3, of which 2 were waited for; matrix products, arithmetic and copies ran while one was open for 16% of the time, Pallas kernels for 0%

commit v1 on v0

v1 whole, which is shorter than its diff:
```python
import functools

import jax
import jax.numpy as jnp
from jax import lax
from jax.experimental import pallas as pl
from jax.experimental.pallas import tpu as pltpu
from jax.sharding import PartitionSpec as P

F32 = jnp.float32
BF16 = jnp.bfloat16
MESH = pl.DeviceIdType.MESH


def nn(x, y):
    return lax.dot_general(x, y, (((1,), (0,)), ((), ())), preferred_element_type=F32)


def nt(x, y):
    return lax.dot_general(x, y, (((1,), (1,)), ((), ())), preferred_element_type=F32)


def tn(x, y):
    return lax.dot_general(x, y, (((0,), (0,)), ((), ())), preferred_element_type=F32)


def kernel(
    ndp, nmp, width, units,
    x_hbm, gain_ref, left_hbm, gate_hbm, right_hbm, cot_hbm,
    out_hbm, sums_hbm,
    x, cot, left, gate, right, dpt, d, hs, y, p, xnt, at, gt, qs,
    grads, arrived, total, rstd, ssx, mux,
    in_sem, wt_sem, out_sem, loc_sem,
    ss_s, ss_r, dp_s, dp_r, h_s, h_r, mu_s, mu_r, rs_s, rs_r, ag_s, ag_r,
):
    nl, rows, blk = x.shape
    me_d, me = lax.axis_index("dp"), lax.axis_index("mp")
    groups = nl // 8

    def cols(ref, i):
        return ref.at[:, pl.ds(pl.multiple_of(i * blk, blk), blk)]

    def fetch_x(i):
        return pltpu.make_async_copy(cols(x_hbm, i), x.at[i], in_sem.at[0, i])

    def fetch_cot(i):
        return pltpu.make_async_copy(cols(cot_hbm, i), cot.at[i], in_sem.at[1, i])

    def loop(n, f):
        def step(i, carry):
            f(i)
            return carry
        lax.fori_loop(0, n, step, 0)

    loop(nl, lambda i: fetch_x(i).start())
    weights = [
        pltpu.make_async_copy(src, dst, wt_sem.at[w])
        for w, (src, dst) in enumerate(((right_hbm, right), (left_hbm, left), (gate_hbm, gate)))
    ]
    weights[0].start()
    loop(nl, lambda i: fetch_cot(i).start())
    weights[1].start()
    weights[2].start()

    def peer_mp(o):
        return (me_d, lax.rem(me + o, nmp))

    def peer_dp(o):
        return (lax.rem(me_d + o, ndp), me)

    barrier = pltpu.get_barrier_semaphore()
    for o in range(1, nmp):
        pl.semaphore_signal(barrier, inc=1, device_id=peer_mp(o), device_id_type=MESH)
    loop(ndp - 1, lambda o: pl.semaphore_signal(
        barrier, inc=1, device_id=peer_dp(o + 1), device_id_type=MESH))

    def remote(src, dst, s, r, dev):
        return pltpu.make_async_remote_copy(
            src_ref=src, dst_ref=dst, send_sem=s, recv_sem=r, device_id=dev, device_id_type=MESH)

    def add_square(i, acc):
        fetch_x(i).wait()
        v = x[i].astype(F32)
        return acc + v * v
    acc = lax.fori_loop(0, nl, add_square, jnp.zeros((rows, blk), F32))
    ssx[0] = jnp.broadcast_to(jnp.sum(acc.T, axis=0, keepdims=True), (8, rows))
    pl.semaphore_wait(barrier, nmp - 1 + ndp - 1)

    def ss_copy(o):
        return remote(ssx.at[0], ssx.at[o], ss_s.at[o], ss_r.at[o], peer_mp(o))
    for o in range(1, nmp):
        ss_copy(o).start()

    weights[0].wait()

    def back_right(k):
        fetch_cot(k).wait()
        dpt[k] = nt(right[k], cot[k]).astype(BF16)
    loop(nl, back_right)

    def dp_copy(o, g):
        dest = lax.rem(me + o, nmp)
        return remote(
            dpt.at[:, pl.ds(pl.multiple_of(16 * (groups * dest + g), 16), 16)],
            d.at[g, pl.ds(nl * me, nl)],
            dp_s.at[o, g], dp_r.at[o, g], peer_mp(o))

    def dp_local(g):
        return pltpu.make_async_copy(
            dpt.at[:, pl.ds(pl.multiple_of(16 * (groups * me + g), 16), 16)],
            d.at[g, pl.ds(nl * me, nl)], loc_sem.at[0, g])
    for g in range(groups):
        for o in range(1, nmp):
            dp_copy(o, g).start()
        dp_local(g).start()

    r = lax.broadcasted_iota(jnp.int32, (128, 128), 0)
    c = lax.broadcasted_iota(jnp.int32, (128, 128), 1)
    moved = ((c & 14) << 3) | ((c >> 4) << 1) | (c & 1)
    swap = jnp.where(r == moved, 1.0, 0.0).astype(BF16)

    for o in range(1, nmp):
        ss_copy(o).wait()
    squares = ssx[0, 0:1]
    for o in range(1, nmp):
        squares = squares + ssx[o, 0:1]
    inv_row = lax.rsqrt(squares / width + 1e-05)
    rstd[...] = jnp.broadcast_to(inv_row, (blk, rows)).T
    weights[1].wait()
    weights[2].wait()

    def forward(i):
        xn = (x[i].astype(F32) * rstd[...] * gain_ref[i]).astype(BF16)
        t = xn.T
        xnt[i] = t
        a = tn(left[i], t)
        v = tn(gate[i], t)
        at[i] = a
        gt[i] = v
        hs[i] = (a * (v / (1.0 + jnp.exp(-v)))).astype(BF16)
    loop(nl, forward)

    nk = y.shape[1]
    for g in range(groups):
        def permute(kk):
            rows16 = pl.ds(pl.multiple_of(16 * kk, 16), 16)
            block = hs[8 * g:8 * g + 8, rows16, :].reshape(128, rows)
            y[g, pl.ds(8 * kk, 8)] = nn(swap, block).astype(BF16).reshape(8, 16, rows)
        loop(nk // 8, permute)

    halves = nl // 8

    def h_copy(o, g, half):
        dest = lax.rem(me + o, nmp)
        return remote(
            y.at[g, pl.ds(nl * dest + 8 * half, 8)],
            p.at[pl.ds(8 * half, 8), pl.ds(pl.multiple_of(16 * (groups * me + g), 16), 16)],
            h_s.at[o, g, half], h_r.at[o, g, half], peer_mp(o))

    def h_local(g, half):
        return pltpu.make_async_copy(
            y.at[g, pl.ds(nl * me + 8 * half, 8)],
            p.at[pl.ds(8 * half, 8), pl.ds(pl.multiple_of(16 * (groups * me + g), 16), 16)],
            loc_sem.at[1 + half, g])
    for half in range(halves):
        for g in range(groups):
            for o in range(1, nmp):
                h_copy(o, g, half).start()
            h_local(g, half).start()

    def rs_copy(u, o):
        off, n = units[u]
        size = n // ndp
        dest = lax.rem(me_d + o, ndp)
        return remote(
            grads.at[pl.ds(pl.multiple_of(off + dest * size, 16), size)],
            arrived.at[o, pl.ds(off // ndp, size)],
            rs_s.at[u, o], rs_r.at[u, o], peer_dp(o))

    def ag_copy(u, o):
        off, n = units[u]
        size = n // ndp
        own = pl.ds(pl.multiple_of(off + me_d * size, 16), size)
        return remote(total.at[own], total.at[own], ag_s.at[u, o], ag_r.at[u, o], peer_dp(o))

    def scatter(u):
        loop(ndp - 1, lambda o: rs_copy(u, o + 1).start())

    def gather(u):
        off, n = units[u]
        size = n // ndp
        own = pl.ds(pl.multiple_of(off + me_d * size, 16), size)

        def add(o, acc):
            rs_copy(u, o + 1).wait()
            return acc + arrived[o + 1, pl.ds(off // ndp, size)].astype(F32)
        acc = lax.fori_loop(0, ndp - 1, add, grads[own].astype(F32))
        total[own] = acc.astype(BF16)
        loop(ndp - 1, lambda o: ag_copy(u, o + 1).start())

    mux[0] = jnp.zeros((8, rows), F32)
    for g in range(groups):
        for o in range(1, nmp):
            dp_copy(o, g).wait()
        dp_local(g).wait()

        def unpermute(kk):
            block = d[g, pl.ds(8 * kk, 8)].reshape(128, rows)
            rows16 = pl.ds(pl.multiple_of(16 * kk, 16), 16)
            hs[8 * g:8 * g + 8, rows16, :] = nn(swap, block).astype(BF16).reshape(8, 16, rows)
        loop(nk // 8, unpermute)

        def backward(j):
            i = 8 * g + j
            dh = hs[i].astype(F32)
            v = gt[i]
            s = 1.0 / (1.0 + jnp.exp(-v))
            da = (dh * (v * s)).astype(BF16)
            dg = (dh * at[i] * s * (1.0 + v * (1.0 - s))).astype(BF16)
            t = xnt[i]
            base = units[g][0]
            grads[pl.ds(pl.multiple_of(base + j * blk, 16), blk)] = nt(t, da).astype(BF16)
            grads[pl.ds(pl.multiple_of(base + (8 + j) * blk, 16), blk)] = nt(t, dg).astype(BF16)
            dxn = nn(left[i], da) + nn(gate[i], dg)
            mux[0] = mux[0] + jnp.sum((dxn * t.astype(F32)).reshape(blk // 8, 8, rows), axis=0)
            qs[i] = cot[i].astype(F32) + rstd[...] * (dxn.T * gain_ref[i])
        loop(8, backward)
        scatter(g)

    def mu_copy(o):
        return remote(mux.at[0], mux.at[o], mu_s.at[o], mu_r.at[o], peer_mp(o))
    for o in range(1, nmp):
        mu_copy(o).start()

    for g in range(groups):
        gather(g)

    for half in range(halves):
        for g in range(groups):
            for o in range(1, nmp):
                h_copy(o, g, half).wait()
            h_local(g, half).wait()
        u = groups + half

        def right_grad(j):
            k = 8 * half + j
            grads[pl.ds(pl.multiple_of(units[u][0] + j * blk, 16), blk)] = nn(p[k], cot[k]).astype(BF16)
        loop(8, right_grad)
        scatter(u)

    for o in range(1, nmp):
        mu_copy(o).wait()
    inner = mux[0]
    for o in range(1, nmp):
        inner = inner + mux[o]
    square = inv_row * inv_row
    factor = jnp.sum(inner, axis=0, keepdims=True) * square / width
    qs_factor = jnp.broadcast_to(factor, (blk, rows)).T

    def store_out(i):
        return pltpu.make_async_copy(x.at[i], cols(out_hbm, i), out_sem.at[i])

    def finish(i):
        x[i] = (qs[i] - x[i].astype(F32) * qs_factor).astype(BF16)
        store_out(i).start()
    loop(nl, finish)

    for half in range(halves):
        gather(groups + half)
    for u in range(len(units)):
        def settle(o):
            ag_copy(u, o + 1).wait()
        loop(ndp - 1, settle)
    sums = pltpu.make_async_copy(total, sums_hbm, wt_sem.at[0])
    sums.start()
    loop(nl, lambda i: store_out(i).wait())
    sums.wait()


def body(samples, gain, left_blocks, gate_blocks, right_blocks, cotangent, *, ndp, nmp):
    rows, width_local = samples.shape
    nl, blk = left_blocks.shape[0], left_blocks.shape[1]
    groups = nl // 8
    nk = nl * nmp
    units = [(g * 16 * blk, 16 * blk) for g in range(groups)]
    units += [(2 * nl * blk + 8 * blk * v, 8 * blk) for v in range(groups)]
    flat = 3 * nl * blk
    dma = pltpu.SemaphoreType.DMA
    any_space = pl.BlockSpec(memory_space=pl.ANY)
    grad_input, sums = pl.pallas_call(
        functools.partial(kernel, ndp, nmp, float(width_local * nmp), units),
        out_shape=(
            jax.ShapeDtypeStruct((rows, width_local), BF16),
            jax.ShapeDtypeStruct((flat, blk), BF16),
        ),
        in_specs=[any_space, pl.BlockSpec(memory_space=pltpu.VMEM)] + [any_space] * 4,
        out_specs=(any_space, any_space),
        scratch_shapes=[
            pltpu.VMEM((nl, rows, blk), BF16),
            pltpu.VMEM((nl, rows, blk), BF16),
            pltpu.VMEM((nl, blk, blk), BF16),
            pltpu.VMEM((nl, blk, blk), BF16),
            pltpu.VMEM((nl, blk, blk), BF16),
            pltpu.VMEM((nl, blk, rows), BF16),
            pltpu.VMEM((groups, nk, 16, rows), BF16),
            pltpu.VMEM((nl, blk, rows), BF16),
            pltpu.VMEM((groups, nk, 16, rows), BF16),
            pltpu.VMEM((nl, blk, rows), BF16),
            pltpu.VMEM((nl, blk, rows), BF16),
            pltpu.VMEM((nl, blk, rows), F32),
            pltpu.VMEM((nl, blk, rows), F32),
            pltpu.VMEM((nl, rows, blk), F32),
            pltpu.VMEM((flat, blk), BF16),
            pltpu.VMEM((ndp, flat // ndp, blk), BF16),
            pltpu.VMEM((flat, blk), BF16),
            pltpu.VMEM((rows, blk), F32),
            pltpu.VMEM((nmp, 8, rows), F32),
            pltpu.VMEM((nmp, 8, rows), F32),
            dma((2, nl)), dma((3,)), dma((nl,)), dma((1 + groups, groups)),
            dma((nmp,)), dma((nmp,)),
            dma((nmp, groups)), dma((nmp, groups)),
            dma((nmp, groups, groups)), dma((nmp, groups, groups)),
            dma((nmp,)), dma((nmp,)),
            dma((2 * groups, ndp)), dma((2 * groups, ndp)),
            dma((2 * groups, ndp)), dma((2 * groups, ndp)),
        ],
        compiler_params=pltpu.CompilerParams(
            collective_id=0, has_side_effects=True, vmem_limit_bytes=60 * 1024 * 1024),
    )(samples, gain.reshape(nl, 1, blk), left_blocks, gate_blocks, right_blocks, cotangent)
    head = sums[:2 * nl * blk].reshape(groups, 2, 8, blk, blk)
    grad_left = head[:, 0].reshape(nl, blk, blk).astype(F32)
    grad_gate = head[:, 1].reshape(nl, blk, blk).astype(F32)
    grad_right = sums[2 * nl * blk:].reshape(nl, blk, blk).astype(F32)
    return grad_input, grad_left, grad_gate, grad_right


def solution(mesh):
    blocks = P("mp", None, None)
    return jax.shard_map(
        functools.partial(body, ndp=mesh.shape["dp"], nmp=mesh.shape["mp"]),
        mesh=mesh,
        in_specs=(P("dp", "mp"), P("mp"), blocks, blocks, blocks, P("dp", "mp")),
        out_specs=(P("dp", "mp"), blocks, blocks, blocks),
        check_vma=False,
    )
```

time: 315 us -> 120 us (0.38)
  the two profiles are of different devices: /device:TPU:0 before, /device:TPU:1 now
where the time goes in v1:
time: 120 us
  Pallas kernels  113 us (94%)
  local copies, waits for them, and re-layouts  4.14 us (3%)
  other arithmetic  2.7 us (2%)
    pallas_call x1, Pallas kernels, body(): pl.pallas_call(functools.partial(kernel, ndp, nmp, float(width_local * nm...  113 us

profile of v1, /device:TPU:1, one launch (start us, length us, event | category | flops | bytes accessed | tf_op | source)
XLA Modules:
  0.0 120.1 jit_solution(8158006840025740716)
XLA Ops:
  0.6 112.5 %shard_map.93 = (bf16[768,2048]{1,0:T(8,128)(2,1)}, bf16[6144,128]{1,0:T(8,128)(2,1)}) custom-call(bf16[768,2048]{1,0:T(8,128)(2,1)} %x_hbm.1, f32[16,1,128]{2,1,0:T(1,128)} %bitcast.12, bf16[16,128,128]{2,1,0:T(8,128)(2,1)} %left_hbm.1, bf16[16,128,128]{2,1,0:T(8,128)(2,1)} %gate_hbm.1, bf16[16,128,128]{2,1,0:T(8,128)(2,1)} %right_hbm.1, ...), custom_call_target="tpu_custom_call" | custom-call | tf_op jit(solution)/shard_map/pallas_call | solution.py:290
  113.2 1.1 slice.15
  114.3 1.3 %slice.12 = bf16[4096,128]{1,0:T(8,128)(2,1)S(1)} slice(bf16[6144,128]{1,0:T(8,128)(2,1)} %get-tuple-element.7), slice={[0:4096], [0:128]} | slice | bytes 2097152 | tf_op jit(solution)/shard_map/slice | solution.py:330
  115.6 0.0 copy-start
  115.6 0.1 fusion
  115.7 1.1 convert.5
  116.8 1.6 %bitcast_convert_fusion = (f32[16,128,128]{2,1,0:T(8,128)}, f32[16,128,128]{2,1,0:T(8,128)}) fusion(bf16[2,1,8,128,128]{4,3,2,1,0:T(8,128)(2,1)S(1)} %get-tuple-element.8, bf16[2,1,8,128,128]{4,3,2,1,0:T(8,128)(2,1)S(1)} %get-tuple-element.9), kind=kLoop, calls=%fused_computation | loop fusion | flops 524288 | bytes 3145728 | tf_op jit(solution)/shard_map/convert_element_type | solution.py:332
  118.4 0.0 copy-done
  118.4 1.7 %copy.11 = bf16[768,2048]{1,0:T(8,128)(2,1)} copy(bf16[768,2048]{1,0:T(8,128)(2,1)S(1)} %copy-done) | data formatting | bytes 6291456
Async XLA Ops:
  115.6 2.8 %copy-start = (bf16[768,2048]{1,0:T(8,128)(2,1)S(1)}, bf16[768,2048]{1,0:T(8,128)(2,1)}, u32[]{:S(2)}) copy-start(bf16[768,2048]{1,0:T(8,128)(2,1)} %get-tuple-element.16) | copy-start | bytes 9437188

commit v2 on v1

v2 whole, which is shorter than its diff:
```python
import functools

import jax
import jax.numpy as jnp
from jax import lax
from jax.experimental import pallas as pl
from jax.experimental.pallas import tpu as pltpu
from jax.sharding import PartitionSpec as P

F32 = jnp.float32
BF16 = jnp.bfloat16
MESH = pl.DeviceIdType.MESH


def nn(x, y):
    return lax.dot_general(x, y, (((1,), (0,)), ((), ())), preferred_element_type=F32)


def nt(x, y):
    return lax.dot_general(x, y, (((1,), (1,)), ((), ())), preferred_element_type=F32)


def tn(x, y):
    return lax.dot_general(x, y, (((0,), (0,)), ((), ())), preferred_element_type=F32)


def kernel(
    ndp, nmp, width, units, direct,
    x_hbm, gain_ref, left_hbm, gate_hbm, right_hbm, cot_hbm,
    out_hbm, left_out, gate_out, right_out,
    x, cot, left, gate, right, dpt, d, hs, y, p, xnt, at, gt, qs,
    grads, arrived, total, rstd, ssx, mux,
    in_sem, wt_sem, out_sem, loc_sem, res_sem,
    ss_s, ss_r, dp_s, dp_r, h_s, h_r, mu_s, mu_r, rs_s, rs_r, ag_s, ag_r,
):
    nl, rows, blk = x.shape
    me_d, me = lax.axis_index("dp"), lax.axis_index("mp")
    groups = nl // 8

    def cols(ref, i):
        return ref.at[:, pl.ds(pl.multiple_of(i * blk, blk), blk)]

    def fetch_x(i):
        return pltpu.make_async_copy(cols(x_hbm, i), x.at[i], in_sem.at[0, i])

    def fetch_cot(i):
        return pltpu.make_async_copy(cols(cot_hbm, i), cot.at[i], in_sem.at[1, i])

    def loop(n, f):
        def step(i, carry):
            f(i)
            return carry
        lax.fori_loop(0, n, step, 0)

    weights = [
        pltpu.make_async_copy(src, dst, wt_sem.at[w])
        for w, (src, dst) in enumerate(((right_hbm, right), (left_hbm, left), (gate_hbm, gate)))
    ]
    weights[0].start()
    loop(nl, lambda i: fetch_cot(i).start())
    loop(nl, lambda i: fetch_x(i).start())
    weights[1].start()
    weights[2].start()

    def peer_mp(o):
        return (me_d, lax.rem(me + o, nmp))

    def peer_dp(o):
        return (lax.rem(me_d + o, ndp), me)

    barrier = pltpu.get_barrier_semaphore()
    for o in range(1, nmp):
        pl.semaphore_signal(barrier, inc=1, device_id=peer_mp(o), device_id_type=MESH)
    loop(ndp - 1, lambda o: pl.semaphore_signal(
        barrier, inc=1, device_id=peer_dp(o + 1), device_id_type=MESH))

    def remote(src, dst, s, r, dev):
        return pltpu.make_async_remote_copy(
            src_ref=src, dst_ref=dst, send_sem=s, recv_sem=r, device_id=dev, device_id_type=MESH)

    weights[0].wait()

    def back_right(k):
        fetch_cot(k).wait()
        dpt[k] = nt(right[k], cot[k]).astype(BF16)
    loop(nl, back_right)

    def dp_copy(o, g):
        dest = lax.rem(me + o, nmp)
        return remote(
            dpt.at[:, pl.ds(pl.multiple_of(16 * (groups * dest + g), 16), 16)],
            d.at[g, pl.ds(nl * me, nl)],
            dp_s.at[o, g], dp_r.at[o, g], peer_mp(o))

    def dp_local(g):
        return pltpu.make_async_copy(
            dpt.at[:, pl.ds(pl.multiple_of(16 * (groups * me + g), 16), 16)],
            d.at[g, pl.ds(nl * me, nl)], loc_sem.at[0, g])
    def send_dp(g):
        for o in range(1, nmp):
            dp_copy(o, g).start()
        dp_local(g).start()
    pl.semaphore_wait(barrier, nmp - 1 + ndp - 1)
    send_dp(0)

    def add_square(i, acc):
        fetch_x(i).wait()
        v = x[i].astype(F32)
        return acc + v * v
    acc = lax.fori_loop(0, nl, add_square, jnp.zeros((rows, blk), F32))
    ssx[0] = jnp.broadcast_to(jnp.sum(acc.T, axis=0, keepdims=True), (8, rows))

    def ss_copy(o):
        return remote(ssx.at[0], ssx.at[o], ss_s.at[o], ss_r.at[o], peer_mp(o))
    for o in range(1, nmp):
        ss_copy(o).start()

    for g in range(1, groups):
        send_dp(g)

    r = lax.broadcasted_iota(jnp.int32, (128, 128), 0)
    c = lax.broadcasted_iota(jnp.int32, (128, 128), 1)
    moved = ((c & 14) << 3) | ((c >> 4) << 1) | (c & 1)
    swap = jnp.where(r == moved, 1.0, 0.0).astype(BF16)

    for o in range(1, nmp):
        ss_copy(o).wait()
    squares = ssx[0, 0:1]
    for o in range(1, nmp):
        squares = squares + ssx[o, 0:1]
    inv_row = lax.rsqrt(squares / width + 1e-05)
    rstd[...] = jnp.broadcast_to(inv_row, (blk, rows)).T
    weights[1].wait()
    weights[2].wait()

    def forward(i):
        xn = (x[i].astype(F32) * rstd[...] * gain_ref[i]).astype(BF16)
        t = xn.T
        xnt[i] = t
        a = tn(left[i], t)
        v = tn(gate[i], t)
        at[i] = a
        gt[i] = v
        hs[i] = (a * (v / (1.0 + jnp.exp(-v)))).astype(BF16)
    loop(nl, forward)

    nk = y.shape[1]
    for g in range(groups):
        def permute(kk):
            rows16 = pl.ds(pl.multiple_of(16 * kk, 16), 16)
            block = hs[8 * g:8 * g + 8, rows16, :].reshape(128, rows)
            y[g, pl.ds(8 * kk, 8)] = nn(swap, block).astype(BF16).reshape(8, 16, rows)
        loop(nk // 8, permute)

    parts = len(units) - groups
    span = nl // parts

    def h_copy(o, g, part):
        dest = lax.rem(me + o, nmp)
        return remote(
            y.at[g, pl.ds(nl * dest + span * part, span)],
            p.at[pl.ds(span * part, span), pl.ds(pl.multiple_of(16 * (groups * me + g), 16), 16)],
            h_s.at[o, g, part], h_r.at[o, g, part], peer_mp(o))

    def h_local(g, part):
        return pltpu.make_async_copy(
            y.at[g, pl.ds(nl * me + span * part, span)],
            p.at[pl.ds(span * part, span), pl.ds(pl.multiple_of(16 * (groups * me + g), 16), 16)],
            loc_sem.at[1 + part, g])

    def send_h(part):
        for g in range(groups):
            for o in range(1, nmp):
                h_copy(o, g, part).start()
            h_local(g, part).start()
    for part in range(parts // 2):
        send_h(part)

    bits = [1 << v for v in range(ndp.bit_length() - 1)]

    def chunk(start, size):
        return pl.ds(pl.multiple_of(start, 16), size)

    def halving(u):
        off, n = units[u]
        stages, lo = [], off
        for v, bit in enumerate(bits):
            size = n >> (v + 1)
            mine = lax.rem(me_d // bit, 2)
            keep, give = lo + mine * size, lo + (1 - mine) * size
            stages.append((v, size, keep, give, (me_d + bit * (1 - 2 * mine), me)))
            lo = keep
        for v, size, keep, give, dev in stages:
            slot = chunk(off + n - 2 * size, size)
            copy = remote(grads.at[chunk(give, size)], arrived.at[slot], rs_s.at[u, v], rs_r.at[u, v], dev)
            copy.start()
            yield
            copy.wait()
            value = (grads[chunk(keep, size)].astype(F32) + arrived[slot].astype(F32)).astype(BF16)
            if v + 1 < len(stages):
                grads[chunk(keep, size)] = value
            else:
                total[chunk(keep, size)] = value
        for v, size, keep, give, dev in reversed(stages):
            held = total.at[chunk(keep, size)]
            copy = remote(held, held, ag_s.at[u, v], ag_r.at[u, v], dev)
            copy.start()
            yield
            copy.wait()

    def straight(u):
        off, n = units[u]
        size = n // ndp
        own = chunk(off + me_d * size, size)

        def rs_copy(o):
            dest = lax.rem(me_d + o, ndp)
            return remote(
                grads.at[chunk(off + dest * size, size)], arrived.at[chunk(off + o * size, size)],
                rs_s.at[u, o], rs_r.at[u, o], peer_dp(o))

        def ag_copy(o):
            return remote(total.at[own], total.at[own], ag_s.at[u, o], ag_r.at[u, o], peer_dp(o))
        loop(ndp - 1, lambda o: rs_copy(o + 1).start())
        yield

        def add(o, acc):
            rs_copy(o + 1).wait()
            return acc + arrived[chunk(off + (o + 1) * size, size)].astype(F32)
        total[own] = lax.fori_loop(0, ndp - 1, add, grads[own].astype(F32)).astype(BF16)
        loop(ndp - 1, lambda o: ag_copy(o + 1).start())
        yield
        loop(ndp - 1, lambda o: ag_copy(o + 1).wait())

    def result_copies(u):
        off, n = units[u]
        if u < groups:
            place = pl.ds(u * n // 2, n // 2)
            return [
                pltpu.make_async_copy(total.at[pl.ds(off, n // 2)], left_out.at[place], res_sem.at[u, 0]),
                pltpu.make_async_copy(total.at[pl.ds(off + n // 2, n // 2)], gate_out.at[place], res_sem.at[u, 1]),
            ]
        return [pltpu.make_async_copy(
            total.at[pl.ds(off, n)], right_out.at[pl.ds((u - groups) * n, n)], res_sem.at[u, 0])]

    running = {}

    def tick(u):
        if u not in running:
            running[u] = straight(u) if u >= len(units) - direct else halving(u)
        try:
            next(running[u])
            return True
        except StopIteration:
            return False

    finished = set()

    def advance():
        for u in sorted(running):
            if u not in finished and not tick(u):
                finished.add(u)
                for copy in result_copies(u):
                    copy.start()

    mux[0] = jnp.zeros((8, rows), F32)
    for g in range(groups):
        for o in range(1, nmp):
            dp_copy(o, g).wait()
        dp_local(g).wait()

        def unpermute(kk):
            block = d[g, pl.ds(8 * kk, 8)].reshape(128, rows)
            rows16 = pl.ds(pl.multiple_of(16 * kk, 16), 16)
            hs[8 * g:8 * g + 8, rows16, :] = nn(swap, block).astype(BF16).reshape(8, 16, rows)
        loop(nk // 8, unpermute)

        def backward(j):
            i = 8 * g + j
            dh = hs[i].astype(F32)
            v = gt[i]
            s = 1.0 / (1.0 + jnp.exp(-v))
            da = (dh * (v * s)).astype(BF16)
            dg = (dh * at[i] * s * (1.0 + v * (1.0 - s))).astype(BF16)
            t = xnt[i]
            base = units[g][0]
            grads[pl.ds(pl.multiple_of(base + j * blk, 16), blk)] = nt(t, da).astype(BF16)
            grads[pl.ds(pl.multiple_of(base + (8 + j) * blk, 16), blk)] = nt(t, dg).astype(BF16)
            dxn = nn(left[i], da) + nn(gate[i], dg)
            mux[0] = mux[0] + jnp.sum((dxn * t.astype(F32)).reshape(blk // 8, 8, rows), axis=0)
            qs[i] = cot[i].astype(F32) + rstd[...] * (dxn.T * gain_ref[i])
        loop(8, backward)
        tick(g)
        if g + 1 < groups:
            advance()

    def mu_copy(o):
        return remote(mux.at[0], mux.at[o], mu_s.at[o], mu_r.at[o], peer_mp(o))
    for o in range(1, nmp):
        mu_copy(o).start()

    for part in range(parts // 2, parts):
        send_h(part)
    advance()
    advance()

    def store_out(i):
        return pltpu.make_async_copy(x.at[i], cols(out_hbm, i), out_sem.at[i])

    def finish_input():
        for o in range(1, nmp):
            mu_copy(o).wait()
        inner = mux[0]
        for o in range(1, nmp):
            inner = inner + mux[o]
        factor = jnp.sum(inner, axis=0, keepdims=True) * (inv_row * inv_row) / width
        factors = jnp.broadcast_to(factor, (blk, rows)).T

        def finish(i):
            x[i] = (qs[i] - x[i].astype(F32) * factors).astype(BF16)
            store_out(i).start()
        loop(nl, finish)

    for part in range(parts):
        if part == parts - 1:
            finish_input()
        for g in range(groups):
            for o in range(1, nmp):
                h_copy(o, g, part).wait()
            h_local(g, part).wait()
        u = groups + part

        def right_grad(j):
            k = span * part + j
            grads[pl.ds(pl.multiple_of(units[u][0] + j * blk, 16), blk)] = nn(p[k], cot[k]).astype(BF16)
        loop(span, right_grad)
        tick(u)
        if part < parts - 1:
            advance()
            if part < parts - 2:
                advance()
    while len(finished) < len(units):
        advance()
    loop(nl, lambda i: store_out(i).wait())
    for u in range(len(units)):
        for copy in result_copies(u):
            copy.wait()


def body(samples, gain, left_blocks, gate_blocks, right_blocks, cotangent, *, ndp, nmp):
    rows, width_local = samples.shape
    nl, blk = left_blocks.shape[0], left_blocks.shape[1]
    groups = nl // 8
    nk = nl * nmp
    units = [(g * 16 * blk, 16 * blk) for g in range(groups)]
    parts = 4
    span = nl // parts * blk
    units += [(2 * nl * blk + span * v, span) for v in range(parts)]
    flat = 3 * nl * blk
    dma = pltpu.SemaphoreType.DMA
    any_space = pl.BlockSpec(memory_space=pl.ANY)
    grad_input, *sums = pl.pallas_call(
        functools.partial(kernel, ndp, nmp, float(width_local * nmp), units, 2),
        out_shape=(
            jax.ShapeDtypeStruct((rows, width_local), BF16),
            *[jax.ShapeDtypeStruct((nl * blk, blk), BF16)] * 3,
        ),
        in_specs=[any_space, pl.BlockSpec(memory_space=pltpu.VMEM)] + [any_space] * 4,
        out_specs=(any_space,) * 4,
        scratch_shapes=[
            pltpu.VMEM((nl, rows, blk), BF16),
            pltpu.VMEM((nl, rows, blk), BF16),
            pltpu.VMEM((nl, blk, blk), BF16),
            pltpu.VMEM((nl, blk, blk), BF16),
            pltpu.VMEM((nl, blk, blk), BF16),
            pltpu.VMEM((nl, blk, rows), BF16),
            pltpu.VMEM((groups, nk, 16, rows), BF16),
            pltpu.VMEM((nl, blk, rows), BF16),
            pltpu.VMEM((groups, nk, 16, rows), BF16),
            pltpu.VMEM((nl, blk, rows), BF16),
            pltpu.VMEM((nl, blk, rows), BF16),
            pltpu.VMEM((nl, blk, rows), F32),
            pltpu.VMEM((nl, blk, rows), F32),
            pltpu.VMEM((nl, rows, blk), F32),
            pltpu.VMEM((flat, blk), BF16),
            pltpu.VMEM((flat, blk), BF16),
            pltpu.VMEM((flat, blk), BF16),
            pltpu.VMEM((rows, blk), F32),
            pltpu.VMEM((nmp, 8, rows), F32),
            pltpu.VMEM((nmp, 8, rows), F32),
            dma((2, nl)), dma((3,)), dma((nl,)), dma((1 + parts, groups)), dma((len(units), 2)),
            dma((nmp,)), dma((nmp,)),
            dma((nmp, groups)), dma((nmp, groups)),
            dma((nmp, groups, parts)), dma((nmp, groups, parts)),
            dma((nmp,)), dma((nmp,)),
            dma((len(units), ndp)), dma((len(units), ndp)),
            dma((len(units), ndp)), dma((len(units), ndp)),
        ],
        compiler_params=pltpu.CompilerParams(
            collective_id=0, has_side_effects=True, vmem_limit_bytes=60 * 1024 * 1024),
    )(samples, gain.reshape(nl, 1, blk), left_blocks, gate_blocks, right_blocks, cotangent)
    grad_left, grad_gate, grad_right = (v.reshape(nl, blk, blk).astype(F32) for v in sums)
    return grad_input, grad_left, grad_gate, grad_right


def solution(mesh):
    blocks = P("mp", None, None)
    return jax.shard_map(
        functools.partial(body, ndp=mesh.shape["dp"], nmp=mesh.shape["mp"]),
        mesh=mesh,
        in_specs=(P("dp", "mp"), P("mp"), blocks, blocks, blocks, P("dp", "mp")),
        out_specs=(P("dp", "mp"), blocks, blocks, blocks),
        check_vma=False,
    )
```

time: 120 us -> 124 us (1.033)
  the two profiles are of different devices: /device:TPU:1 before, /device:TPU:0 now
where the time goes in v2:
time: 124 us
  Pallas kernels  115 us (93%)
  other arithmetic  6.5 us (5%)
  local copies, waits for them, and re-layouts  1.67 us (1%)
    pallas_call x1, Pallas kernels, body(): pl.pallas_call(functools.partial(kernel, ndp, nmp, float(width_local * nm...  115 us
    convert_element_type x3, other arithmetic, body(): v.reshape(nl, blk, blk).astype(F32)  6.5 us

profile of v2, /device:TPU:0, one launch (start us, length us, event | category | flops | bytes accessed | tf_op | source)
XLA Modules:
  0.0 123.5 jit_solution(13410365248552369115)
XLA Ops:
  0.6 114.7 %shard_map.93 = (bf16[768,2048]{1,0:T(8,128)(2,1)}, bf16[2048,128]{1,0:T(8,128)(2,1)}, bf16[2048,128]{1,0:T(8,128)(2,1)}, bf16[2048,128]{1,0:T(8,128)(2,1)}) custom-call(bf16[768,2048]{1,0:T(8,128)(2,1)} %x_hbm.1, f32[16,1,128]{2,1,0:T(1,128)} %bitcast.10, bf16[16,128,128]{2,1,0:T(8,128)(2,1)} %left_hbm.1, bf16[16,128,128]{2,1,0:T(8,128)(2,1)} %gate_hbm.1, ...), custom_call_target="tpu_custom_call" | custom-call | tf_op jit(solution)/shard_map/pallas_call | solution.py:362
  115.4 0.0 copy-start
  115.4 2.3 %convert.3 = f32[16,128,128]{2,1,0:T(8,128)} convert(bf16[16,128,128]{2,1,0:T(8,128)(2,1)} %bitcast.9) | non-fusion elementwise | flops 262144 | bytes 1572864 | tf_op jit(solution)/shard_map/convert_element_type | solution.py:402
  117.6 2.1 %convert.4 = f32[16,128,128]{2,1,0:T(8,128)} convert(bf16[16,128,128]{2,1,0:T(8,128)(2,1)} %bitcast.8) | non-fusion elementwise | flops 262144 | bytes 1572864 | tf_op jit(solution)/shard_map/convert_element_type | solution.py:402
  119.8 2.1 %convert.5 = f32[16,128,128]{2,1,0:T(8,128)} convert(bf16[16,128,128]{2,1,0:T(8,128)(2,1)} %bitcast.7) | non-fusion elementwise | flops 262144 | bytes 1572864 | tf_op jit(solution)/shard_map/convert_element_type | solution.py:402
  121.9 0.0 copy-done
  121.9 1.7 %copy.11 = bf16[768,2048]{1,0:T(8,128)(2,1)} copy(bf16[768,2048]{1,0:T(8,128)(2,1)S(1)} %copy-done) | data formatting | bytes 6291456
Async XLA Ops:
  115.4 6.5 %copy-start = (bf16[768,2048]{1,0:T(8,128)(2,1)S(1)}, bf16[768,2048]{1,0:T(8,128)(2,1)}, u32[]{:S(2)}) copy-start(bf16[768,2048]{1,0:T(8,128)(2,1)} %get-tuple-element.16) | copy-start | bytes 9437188
